TPU v7x, 256 devices: a whole 4x4x8 slice. The times are simulated.
256 devices in a mesh: samp: 16 (over z, x_lo), tok: 16 (over x_hi, y, core).
Axes of the slice: x: 4 (x_hi: 2, x_lo: 2; x = x_hi * 2 + x_lo), y: 4, z: 8, core: 2. Of those that a mesh axis runs over, the one named last changes fastest.
Arguments:
- features_in: bfloat16 [16, 256, 512, 128], P('samp', 'tok'), may hold values from -6 to 6
- path_noise: bfloat16 [16, 256, 512, 128], P('samp', 'tok'), may hold values from -6 to 6
- latent: float32 [16, 512], P('samp'), may hold values from -6 to 6
- bank: bfloat16 [8, 9, 128, 128], replicated, may hold values from -0.1875 to 0.1875
- style_weight: float32 [512, 128], replicated, may hold values from -0.25 to 0.25
- select_weight: float32 [512, 8], replicated, may hold values from -0.25 to 0.25
- path_mean: float32 [1], replicated, may hold values from 0.5 to 2
Outputs:
- features: bfloat16 [16, 256, 512, 128], P('samp', 'tok')
- penalty: float32 [16], P('samp')
- bank_grad: float32 [8, 9, 128, 128], P(None, None, 'samp')
- style_grad: float32 [512, 128], replicated
- select_grad: float32 [512, 8], replicated
All inputs are finite; a program needn't handle non-finite values.
Results may differ from a plain program's by a relative error of at most 0.0049.
Values may be sent and summed in bfloat16 or wider, within the bound.
No kernel may reach another device: no remote copies, remote signals or barrier semaphores. Data moves between devices by JAX's collectives and lax.ppermute only.
A program may use at most 128 MiB of HBM per device.

v0:
```python
import math
import jax
import jax.numpy as jnp
from jax import lax
from jax.sharding import PartitionSpec as P

HIGH = lax.Precision.HIGHEST


def with_halo(block, sides, width):
    for axis, dim in sides:
        count = lax.axis_size(axis)
        forward = [(i, i + 1) for i in range(count - 1)]
        backward = [(target, source) for source, target in forward]
        low = lax.ppermute(
            lax.slice_in_dim(block, block.shape[dim] - width, None, axis=dim), axis, forward
        )
        high = lax.ppermute(lax.slice_in_dim(block, 0, width, axis=dim), axis, backward)
        block = jnp.concatenate([low, block, high], axis=dim)
    return block


def mixing(wvec, select_w):
    logits = jnp.dot(wvec, select_w, precision=HIGH)
    expo = jnp.exp(logits)
    return expo / jnp.sum(expo)


def modulate(wvec, kern, style_w):
    style = jnp.dot(wvec, style_w, precision=HIGH) + 1.0
    scaled = kern * style[None, :, None]
    demod = lax.rsqrt(jnp.sum(scaled * scaled, axis=(0, 1)) + 1e-08)
    return scaled * demod[None, None, :]


def kernel_of(wvec, bank32, style_w, select_w):
    mixed = jnp.einsum("b,bkio->kio", mixing(wvec, select_w), bank32, precision=HIGH)
    return modulate(wvec, mixed, style_w)


def path_grad(wvec, corr_one, bank32, style_w, select_w):
    return jax.grad(lambda v: jnp.sum(corr_one * kernel_of(v, bank32, style_w, select_w)))(wvec)


def penalty_of(wvec, corr_one, bank32, style_w, select_w, target):
    grad_w = path_grad(wvec, corr_one, bank32, style_w, select_w)
    length = jnp.sqrt(jnp.sum(grad_w * grad_w) + 1e-08)
    return (length - target) ** 2


def local(features_in, path_noise, latent, bank, style_weight, select_weight, path_mean):
    count, rows, cols, chans = features_in.shape
    images = count * lax.axis_size("samp")
    height = rows * lax.axis_size("tok")
    padded_rows = with_halo(features_in, (("tok", 1),), 1)
    padded = jnp.pad(padded_rows, ((0, 0), (0, 0), (1, 1), (0, 0)))
    bank32 = bank.astype(jnp.float32)
    kernels = jax.vmap(kernel_of, (0, None, None, None))(
        latent, bank32, style_weight, select_weight
    )
    kernel_low = kernels.astype(jnp.bfloat16)
    total = jnp.zeros((count, rows, cols, chans), jnp.float32)
    corr_taps = []
    for tap in range(9):
        ky, kx = (tap // 3, tap % 3)
        window = padded[:, ky : ky + rows, kx : kx + cols, :]
        total = total + jnp.einsum(
            "nrci,nio->nrco", window, kernel_low[:, tap], preferred_element_type=jnp.float32
        )
        corr_taps.append(
            jnp.einsum("nrci,nrco->nio", window, path_noise, preferred_element_type=jnp.float32)
        )
    features = total.astype(jnp.bfloat16)
    corr_local = jnp.stack(corr_taps, 1)
    corr = lax.psum(corr_local, "tok") * (1.0 / math.sqrt(height * cols))
    target = path_mean[0]
    weights = jnp.full((count,), 1.0 / images, jnp.float32)

    def pens_fn(bank_f, style_w, select_w):
        return jax.vmap(penalty_of, (0, 0, None, None, None, None))(
            latent, corr, bank_f, style_w, select_w, target
        )

    pens, back = jax.vjp(pens_fn, bank32, style_weight, select_weight)
    bank_part, style_part, select_part = back(weights)
    bank_grad = lax.psum_scatter(bank_part, "samp", scatter_dimension=2, tiled=True)
    style_grad, select_grad = lax.psum((style_part, select_part), "samp")
    return (features, pens, bank_grad, style_grad, select_grad)


def solution(mesh):
    placed = (
        P("samp", "tok", None, None),
        P("samp", "tok", None, None),
        P("samp", None),
        P(),
        P(),
        P(),
        P(),
    )
    return jax.shard_map(
        local,
        mesh=mesh,
        in_specs=placed,
        out_specs=(P("samp", "tok", None, None), P("samp"), P(None, None, "samp", None), P(), P()),
        check_vma=False,
    )
```

profile of v0, /device:TPU:16, one launch (start us, length us, event | category | flops | bytes accessed | tf_op | source)
XLA Modules:
  0.0 468.9 jit_solution(189163393301264175)
XLA Ops:
  8.4 1.9 collective-permute-start
  10.3 3.6 collective-permute-start.1
  18.7 2.8 fusion.10
  32.1 2.8 fusion.47
  35.2 134.9 %all-reduce.4.cloned.1.call-done = f32[1,9,128,128]{3,2,1,0:T(8,128)} async-done(((f32[1,9,128,128]{3,2,1,0:T(8,128)}), f32[1,9,128,128]{3,2,1,0:T(8,128)}) %all-reduce.4.cloned.1.call-update) | async-done | bytes 589840 | tf_op jit(solution)/shard_map/psum | solution.py:75
  174.1 7.3 %multiply_reduce_fusion.9 = (f32[]{:T(128)}, f32[8]{0:T(128)}) fusion(f32[8]{0:T(128)} %copy-done.26, f32[]{:T(128)} %bitcast.70, f32[9,128,128,1]{2,3,1,0:T(1,128)S(1)} %bitcast.363, bf16[8,9,128,128]{3,2,1,0:T(8,128)(2,1)S(1)} %copy-done), kind=kOutput, calls=%fused_computation.137 | convolution fusion | flops 14155799 | bytes 2949192 | tf_op jit(solution)/shard_map/jvp(vmap(transpose(jvp(b,bkio->kio))))/dot_general | solution.py:37
  188.0 1.8 convolution_bitcast_fusion
  189.7 1.9 multiply_reduce_fusion.10
  193.6 2.8 fusion.43
  196.4 1.7 multiply_reduce_fusion
  201.0 3.4 multiply_add_fusion
  206.6 6.2 %multiply_reduce_fusion.7 = (f32[]{:T(128)}, f32[]{:T(128)}, f32[]{:T(128)}, f32[8]{0:T(128)S(1)}) fusion(f32[8]{0:T(128)S(1)} %copy-done.39, f32[8]{0:T(128)S(1)} %copy-done.27, f32[]{:T(128)S(6)} %neg.23, f32[]{:T(128)S(6)} %div.81, f32[8]{0:T(128)S(1)} %copy-done.36, f32[9,128,128,1]{2,3,1,0:T(1,128)S(1)} %bitcast.366, ...), kind=kOutput, calls=%fused_computation.133 | convolution fusion | flops 14155853 | bytes 2949268 | tf_op jit(solution)/shard_map/transpose(jvp(vmap(jvp(b,bkio->kio))))/dot_general | solution.py:37
  215.4 63.8 %psum.23 = f32[512,8]{0,1:T(8,128)} all-reduce(f32[512,8]{0,1:T(8,128)S(1)} %bitcast_add_fusion.3), channel_id=1, replica_groups=mesh['samp'=16,'tok'=16] {'samp'}, use_global_device_ids=true, to_apply=%region_17.18 | all-reduce | flops 4096 | bytes 32768 | tf_op jit(solution)/shard_map/psum | solution.py:87
  279.2 2.4 fusion.53
  281.6 2.7 fusion.50
  284.4 2.7 fusion.39
  287.1 2.6 fusion.38
  289.7 2.7 fusion.33
  292.4 2.7 fusion.37
  295.1 2.7 fusion.36
  297.8 2.7 fusion.35
  300.5 11.8 %fusion.11 = bf16[1,16,512,128]{3,2,1,0:T(8,128)(2,1)} fusion(f32[16,512,128]{2,1,0:T(8,128)S(1)} %fusion.53, f32[16,512,128]{2,1,0:T(8,128)} %fusion.39, f32[16,512,128]{2,1,0:T(8,128)} %fusion.38, f32[128,16,512]{0,2,1:T(8,128)} %fusion.33, f32[16,512,128]{2,1,0:T(8,128)} %fusion.37, f32[16,512,128]{2,1,0:T(8,128)} %fusion.36, ...), kind=kOutput, calls=%fused_computation.15 | convolution fusion | flops 277872640 | bytes 37781504 | tf_op jit(solution)/shard_map/nrci,nio->nrco/dot_general | solution.py:67
  312.4 33.8 %all-reduce.6.cloned.1.call-done = f32[512,128]{1,0:T(8,128)} async-done(((f32[512,128]{1,0:T(8,128)}), f32[512,128]{1,0:T(8,128)}) %all-reduce.6.cloned.1.call-update) | async-done | bytes 262160 | tf_op jit(solution)/shard_map/psum | solution.py:87
  346.2 113.4 %reduce-scatter.2.cloned.1.call-done = f32[8,9,8,128]{3,2,1,0:T(8,128)} async-done(((f32[8,9,128,128]{3,2,1,0:T(8,128)}), f32[8,9,8,128]{3,2,1,0:T(8,128)}) %reduce-scatter.2.cloned.1.call-update) | async-done | bytes 294928 | tf_op jit(solution)/shard_map/reduce_scatter | solution.py:86
  (123 shorter events, 30.2 us)
Async XLA Ops:
  7.2 24.9 %copy-start = (bf16[8,9,128,128]{3,2,1,0:T(8,128)(2,1)S(1)}, bf16[8,9,128,128]{3,2,1,0:T(8,128)(2,1)}, u32[]{:S(2)}) copy-start(bf16[8,9,128,128]{3,2,1,0:T(8,128)(2,1)} %param.10) | copy-start | bytes 7077892
  7.2 162.9 %all-reduce.4.cloned.1.call-start = ((), (), s32[]{:S(2)}) async-start(), calls=%async_computation.1 | async-start | bytes 1179648 | tf_op jit(solution)/shard_map/psum | solution.py:75
  8.4 10.3 %collective-permute-start = (bf16[1,1,512,128]{3,2,1,0:T(8,128)(2,1)S(1)}, bf16[1,1,512,128]{3,2,1,0:T(8,128)(2,1)S(1)}, u32[]{:S(2)}, u32[]{:S(2)}) collective-permute-start(bf16[1,1,512,128]{3,2,1,0:T(8,128)(2,1)S(1)} %get-tuple-element.15), channel_id=1, source_target_pairs={{0,1},{1,2},{2,3},{3,4},{4,5},{5,6},{6,7},{7,8},{8,9},{9,10},{10,1... | collective-permute-start | bytes 393224 | tf_op jit(solution)/shard_map/ppermute | solution.py:15
  10.3 8.4 %collective-permute-start.1 = (bf16[1,1,512,128]{3,2,1,0:T(8,128)(2,1)S(1)}, bf16[1,1,512,128]{3,2,1,0:T(8,128)(2,1)S(1)}, u32[]{:S(2)}, u32[]{:S(2)}) collective-permute-start(bf16[1,1,512,128]{3,2,1,0:T(8,128)(2,1)S(1)} %get-tuple-element.16), channel_id=1, source_target_pairs={{1,0},{2,1},{3,2},{4,3},{5,4},{6,5},{7,6},{8,7},{9,8},{10,9},{11,1... | collective-permute-start | bytes 393224 | tf_op jit(solution)/shard_map/ppermute | solution.py:18
  16.2 15.3 %copy-start.26 = (f32[8]{0:T(128)}, f32[8]{0:T(128)S(1)}, u32[]{:S(2)}) copy-start(f32[8]{0:T(128)S(1)} %get-tuple-element.26) | copy-start | bytes 100
  18.7 153.3 %copy-start.20 = (f32[128]{0:T(128)}, f32[128]{0:T(128)S(1)}, u32[]{:S(2)}) copy-start(f32[128]{0:T(128)S(1)} %fusion.128) | copy-start | bytes 1540
  18.7 2.9 copy-start.10
  18.7 3.7 copy-start.13
  18.7 10.0 %copy-start.15 = (bf16[1,1,512,128]{3,2,1,0:T(8,128)(2,1)}, bf16[1,1,512,128]{3,2,1,0:T(8,128)(2,1)S(1)}, u32[]{:S(2)}) copy-start(bf16[1,1,512,128]{3,2,1,0:T(8,128)(2,1)S(1)} %collective-permute-done.1) | copy-start | bytes 393220
  21.6 8.0 %copy-start.1 = (bf16[1,18,514,128]{3,2,1,0:T(8,128)(2,1)}, bf16[1,18,514,128]{3,2,1,0:T(8,128)(2,1)S(1)}, u32[]{:S(2)}) copy-start(bf16[1,18,514,128]{3,2,1,0:T(8,128)(2,1)S(1)} %fusion.10) | copy-start | bytes 7105540
  31.2 315.0 %all-reduce.6.cloned.1.call-start = ((), (), s32[]{:S(2)}) async-start(), calls=%async_computation.3 | async-start | bytes 524288 | tf_op jit(solution)/shard_map/psum | solution.py:87
  32.1 2.8 copy-start.37
  35.1 136.8 %copy-start.30 = (f32[128]{0:T(128)}, f32[128]{0:T(128)S(1)}, u32[]{:S(2)}) copy-start(f32[128]{0:T(128)S(1)} %multiply_reduce_fusion.4) | copy-start | bytes 1540
  173.2 10.8 %copy-start.6 = (f32[1,9,128,128]{3,2,1,0:T(8,128)}, f32[1,9,128,128]{3,2,1,0:T(8,128)S(1)}, u32[]{:S(2)}) copy-start(f32[1,9,128,128]{3,2,1,0:T(8,128)S(1)} %get-tuple-element.14) | copy-start | bytes 1769476
  173.3 10.1 %copy-start.17 = (f32[512,8]{0,1:T(8,128)S(1)}, f32[512,8]{0,1:T(8,128)}, u32[]{:S(2)}) copy-start(f32[512,8]{0,1:T(8,128)} %param.12) | copy-start | bytes 49156
  188.0 3.7 copy-start.18
  188.0 10.2 %copy-start.5 = (f32[1,9,128,128]{3,2,1,0:T(8,128)S(1)}, f32[1,9,128,128]{3,2,1,0:T(8,128)}, u32[]{:S(2)}) copy-start(f32[1,9,128,128]{3,2,1,0:T(8,128)} %all-reduce.4.cloned.1.call-done) | copy-start | bytes 1769476
  191.7 4.8 %copy-start.25 = (f32[128]{0:T(128)S(1)}, f32[128]{0:T(128)}, u32[]{:S(2)}) copy-start(f32[128]{0:T(128)} %convolution_bitcast_fusion) | copy-start | bytes 1540
  196.4 2.7 copy-start.21
  201.0 258.6 %reduce-scatter.2.cloned.1.call-start = ((), (), s32[]{:S(2)}) async-start(), calls=%async_computation.2 | async-start | bytes 5013504 | tf_op jit(solution)/shard_map/reduce_scatter | solution.py:86
  204.5 10.9 %copy-start.35 = (f32[8]{0:T(128)S(1)}, f32[8]{0:T(128)}, u32[]{:S(2)}) copy-start(f32[8]{0:T(128)} %copy-done.34) | copy-start | bytes 100
  204.5 74.7 %copy-start.11 = (bf16[1,9,128,128]{3,2,1,0:T(8,128)(2,1)S(1)}, bf16[1,9,128,128]{3,2,1,0:T(8,128)(2,1)}, u32[]{:S(2)}) copy-start(bf16[1,9,128,128]{3,2,1,0:T(8,128)(2,1)} %get-tuple-element.18) | copy-start | bytes 884740
  204.5 74.7 %copy-start.16 = (bf16[1,1,512,128]{3,2,1,0:T(8,128)(2,1)S(1)}, bf16[1,1,512,128]{3,2,1,0:T(8,128)(2,1)}, u32[]{:S(2)}) copy-start(bf16[1,1,512,128]{3,2,1,0:T(8,128)(2,1)} %copy-done.15) | copy-start | bytes 393220
  281.6 2.7 copy-start.2
  (22 other events, 36.4 us)
Sparse Core Ops, SparseCore 0:
  31.3 138.6 all-reduce.3
  201.1 145.0 all-reduce.5
  349.3 110.2 reduce-scatter.1
where the time goes:
time: 470 us; the launch traced here: 469 us
  waiting for transfers between devices  282 us (60%)
  matrix products  67.1 us (14%)
  blocking collectives  63.8 us (14%)
  between operations  23.4 us (5%)
  other arithmetic  19.4 us (4%)
  local copies, waits for them, and re-layouts  7.22 us (2%)
  starting transfers between devices  5.86 us (1%)
    psum x1, waiting for transfers between devices, local(): corr = lax.psum(corr_local, 'tok') * (1.0 / math.sqrt(height * cols))  135 us
    reduce_scatter x1, waiting for transfers between devices, local(): lax.psum_scatter(bank_part, 'samp', scatter_dimension=2, tiled=True)  113 us
    psum x1, blocking collectives, local(): style_grad, select_grad = lax.psum((style_part, select_part), 'samp')  63.8 us
    psum x1, waiting for transfers between devices, local(): style_grad, select_grad = lax.psum((style_part, select_part), 'samp')  33.8 us
    dot_general x9, matrix products, local(): jnp.einsum('nrci,nio->nrco', window, kernel_low[:, tap], preferred_elemen...  33.1 us
    dot_general x4, matrix products, kernel_of(): jnp.einsum('b,bkio->kio', mixing(wvec, select_w), bank32, precision=HIGH)  19.1 us
  transfers between devices with their start and end apart: 5, of which 3 were waited for; matrix products, arithmetic and copies ran while one was open for 11% of the time, Pallas kernels for 0%

commit v1 on v0

--- a/solution.py
+++ b/solution.py
@@ -72,7 +72,7 @@
         )
     features = total.astype(jnp.bfloat16)
     corr_local = jnp.stack(corr_taps, 1)
-    corr = lax.psum(corr_local, "tok") * (1.0 / math.sqrt(height * cols))
+    corr = jnp.sum(lax.all_gather(corr_local, "tok"), axis=0) * (1.0 / math.sqrt(height * cols))
     target = path_mean[0]
     weights = jnp.full((count,), 1.0 / images, jnp.float32)
 

time: 470 us -> 409 us (0.87)
  waiting for transfers between devices: 282 us -> 221 us
    psum x1 -> x0, waiting for transfers between devices: 135 us -> none  [local(): corr = lax.psum(corr_local, 'tok') * (1.0 / math.sqrt(height * cols))]
    all_gather x0 -> x1, waiting for transfers between devices: none -> 80.1 us  [local(): lax.all_gather(corr_local, 'tok')]
    psum x1, waiting for transfers between devices: 33.8 us -> 24.3 us  [local(): style_grad, select_grad = lax.psum((style_part, select_part), 'samp')]
  transfers between devices with their start and end apart: 5 -> 5, of which waited for: 3 -> 5; matrix products, arithmetic and copies ran while one was open for 11% -> 12% of each run, Pallas kernels for 0% -> 0%
where the time goes in v1:
time: 409 us; the launch traced here: 408 us
  waiting for transfers between devices  221 us (54%)
  matrix products  65.1 us (16%)
  blocking collectives  63 us (15%)
  between operations  23.3 us (6%)
  other arithmetic  22.4 us (5%)
  local copies, waits for them, and re-layouts  7.42 us (2%)
  starting transfers between devices  6 us (1%)
    reduce_scatter x1, waiting for transfers between devices, local(): lax.psum_scatter(bank_part, 'samp', scatter_dimension=2, tiled=True)  114 us
    all_gather x1, waiting for transfers between devices, local(): lax.all_gather(corr_local, 'tok')  80.1 us
    psum x1, blocking collectives, local(): style_grad, select_grad = lax.psum((style_part, select_part), 'samp')  63 us
    dot_general x9, matrix products, local(): jnp.einsum('nrci,nio->nrco', window, kernel_low[:, tap], preferred_elemen...  33.1 us
    psum x1, waiting for transfers between devices, local(): style_grad, select_grad = lax.psum((style_part, select_part), 'samp')  24.3 us
    dot_general x4, matrix products, kernel_of(): jnp.einsum('b,bkio->kio', mixing(wvec, select_w), bank32, precision=HIGH)  18.4 us
  transfers between devices with their start and end apart: 5, of which 5 were waited for; matrix products, arithmetic and copies ran while one was open for 12% of the time, Pallas kernels for 0%

profile of v1, /device:TPU:16, one launch (start us, length us, event | category | flops | bytes accessed | tf_op | source)
XLA Modules:
  0.0 407.8 jit_solution(15561334558939247863)
XLA Ops:
  8.4 1.9 collective-permute-start
  10.3 3.8 collective-permute-start.1
  14.7 1.9 collective-permute-done.1
  16.6 2.7 fusion.10
  33.4 2.8 fusion.47
  36.2 80.1 %all-gather.3.cloned.1.call-done = f32[16,9,128,128]{3,2,1,0:T(8,128)} async-done(((f32[1,9,128,128]{3,2,1,0:T(8,128)}), f32[16,9,128,128]{3,2,1,0:T(8,128)}) %all-gather.3.cloned.1.call-update) | async-done | bytes 9437200 | tf_op jit(solution)/shard_map/all_gather | solution.py:75
  116.3 4.4 %reduce.29 = f32[9,128,128]{2,1,0:T(8,128)S(1)} reduce(f32[16,9,128,128]{3,2,1,0:T(8,128)} %all-gather.3.cloned.1.call-done, f32[]{:T(128)} %constant.11.clone.1), dimensions={0}, to_apply=%region_2.3 | reduce | flops 2211840 | bytes 10027012 | tf_op jit(solution)/shard_map/reduce_sum | solution.py:75
  124.5 6.7 %multiply_reduce_fusion.11 = (f32[]{:T(128)}, f32[8]{0:T(128)}) fusion(f32[8]{0:T(128)S(1)} %copy-done.25, f32[]{:T(128)} %bitcast.66, f32[9,128,128,1]{2,3,1,0:T(1,128)S(1)} %bitcast.336, bf16[8,9,128,128]{3,2,1,0:T(8,128)(2,1)S(1)} %copy-done), kind=kOutput, calls=%fused_computation.135 | convolution fusion | flops 14155799 | bytes 2949192 | tf_op jit(solution)/shard_map/jvp(vmap(transpose(jvp(b,bkio->kio))))/dot_general | solution.py:37
  139.6 1.9 multiply_reduce_fusion.12
  143.5 2.8 fusion.43
  149.5 4.1 %multiply_add_fusion = f32[8,9,128,128]{3,2,1,0:T(8,128)} fusion(f32[9,128,128]{2,1,0:T(8,128)} %get-tuple-element.19, f32[8]{0:T(128)} %copy-done.37, f32[9,128,128]{2,1,0:T(8,128)} %copy-done.8, f32[8]{0:T(128)S(1)} %divide_add_fusion.1), kind=kLoop, calls=%fused_computation.3 | loop fusion | flops 3538944 | bytes 5898304 | tf_op jit(solution)/shard_map/transpose(jvp(vmap(jvp(b,bkio->kio))))/add_any | solution.py:37
  155.7 6.1 %multiply_reduce_fusion.9 = (f32[]{:T(128)}, f32[]{:T(128)}, f32[]{:T(128)}, f32[8]{0:T(128)S(1)}) fusion(f32[8]{0:T(128)S(1)} %copy-done.39, f32[8]{0:T(128)S(1)} %copy-done.26, f32[]{:T(128)S(6)} %neg.23, f32[]{:T(128)S(6)} %div.81, f32[8]{0:T(128)S(1)} %copy-done.35, f32[9,128,128,1]{2,3,1,0:T(1,128)S(1)} %bitcast.335, ...), kind=kOutput, calls=%fused_computation.131 | convolution fusion | flops 14155853 | bytes 2949268 | tf_op jit(solution)/shard_map/transpose(jvp(vmap(jvp(b,bkio->kio))))/dot_general | solution.py:37
  164.4 63.0 %psum.15 = f32[512,8]{0,1:T(8,128)} all-reduce(f32[512,8]{0,1:T(8,128)S(1)} %bitcast_add_fusion.2), channel_id=1, replica_groups=mesh['samp'=16,'tok'=16] {'samp'}, use_global_device_ids=true, to_apply=%region_17.18 | all-reduce | flops 4096 | bytes 32768 | tf_op jit(solution)/shard_map/psum | solution.py:87
  227.5 2.4 fusion.53
  229.9 2.7 fusion.50
  232.6 2.7 fusion.39
  235.3 2.6 fusion.38
  238.0 2.7 fusion.33
  240.6 2.7 fusion.37
  243.4 2.7 fusion.36
  246.1 2.7 fusion.35
  248.8 11.8 %fusion.11 = bf16[1,16,512,128]{3,2,1,0:T(8,128)(2,1)} fusion(f32[16,512,128]{2,1,0:T(8,128)S(1)} %fusion.53, f32[16,512,128]{2,1,0:T(8,128)} %fusion.39, f32[16,512,128]{2,1,0:T(8,128)} %fusion.38, f32[128,16,512]{0,2,1:T(8,128)} %fusion.33, f32[16,512,128]{2,1,0:T(8,128)} %fusion.37, f32[16,512,128]{2,1,0:T(8,128)} %fusion.36, ...), kind=kOutput, calls=%fused_computation.15 | convolution fusion | flops 277872640 | bytes 37781504 | tf_op jit(solution)/shard_map/nrci,nio->nrco/dot_general | solution.py:67
  260.6 24.3 %all-reduce.3.cloned.1.call-done = f32[512,128]{1,0:T(8,128)} async-done(((f32[512,128]{1,0:T(8,128)}), f32[512,128]{1,0:T(8,128)}) %all-reduce.3.cloned.1.call-update) | async-done | bytes 262160 | tf_op jit(solution)/shard_map/psum | solution.py:87
  284.9 113.6 %reduce-scatter.2.cloned.1.call-done = f32[8,9,8,128]{3,2,1,0:T(8,128)} async-done(((f32[8,9,128,128]{3,2,1,0:T(8,128)}), f32[8,9,8,128]{3,2,1,0:T(8,128)}) %reduce-scatter.2.cloned.1.call-update) | async-done | bytes 294928 | tf_op jit(solution)/shard_map/reduce_scatter | solution.py:86
  (121 shorter events, 31.2 us)
Async XLA Ops:
  7.2 26.2 %copy-start = (bf16[8,9,128,128]{3,2,1,0:T(8,128)(2,1)S(1)}, bf16[8,9,128,128]{3,2,1,0:T(8,128)(2,1)}, u32[]{:S(2)}) copy-start(bf16[8,9,128,128]{3,2,1,0:T(8,128)(2,1)} %param.10) | copy-start | bytes 7077892
  7.2 109.1 %all-gather.3.cloned.1.call-start = ((), (), s32[]{:S(2)}) async-start(), calls=%async_computation.3 | async-start | bytes 10027008 | tf_op jit(solution)/shard_map/all_gather | solution.py:75
  8.4 6.3 %collective-permute-start = (bf16[1,1,512,128]{3,2,1,0:T(8,128)(2,1)S(1)}, bf16[1,1,512,128]{3,2,1,0:T(8,128)(2,1)S(1)}, u32[]{:S(2)}, u32[]{:S(2)}) collective-permute-start(bf16[1,1,512,128]{3,2,1,0:T(8,128)(2,1)S(1)} %get-tuple-element.20), channel_id=1, source_target_pairs={{0,1},{1,2},{2,3},{3,4},{4,5},{5,6},{6,7},{7,8},{8,9},{9,10},{10,1... | collective-permute-start | bytes 393224 | tf_op jit(solution)/shard_map/ppermute | solution.py:15
  10.3 9.0 %copy-start.10 = (bf16[1,16,512,128]{3,2,1,0:T(8,128)(2,1)S(1)}, bf16[1,16,512,128]{3,2,1,0:T(8,128)(2,1)}, u32[]{:S(2)}) copy-start(bf16[1,16,512,128]{3,2,1,0:T(8,128)(2,1)} %param.8) | copy-start | bytes 6291460
  10.3 6.3 %collective-permute-start.1 = (bf16[1,1,512,128]{3,2,1,0:T(8,128)(2,1)S(1)}, bf16[1,1,512,128]{3,2,1,0:T(8,128)(2,1)S(1)}, u32[]{:S(2)}, u32[]{:S(2)}) collective-permute-start(bf16[1,1,512,128]{3,2,1,0:T(8,128)(2,1)S(1)} %get-tuple-element.21), channel_id=1, source_target_pairs={{1,0},{2,1},{3,2},{4,3},{5,4},{6,5},{7,6},{8,7},{9,8},{10,9},{11,1... | collective-permute-start | bytes 393224 | tf_op jit(solution)/shard_map/ppermute | solution.py:18
  14.7 5.5 %copy-start.13 = (bf16[1,1,512,128]{3,2,1,0:T(8,128)(2,1)}, bf16[1,1,512,128]{3,2,1,0:T(8,128)(2,1)S(1)}, u32[]{:S(2)}) copy-start(bf16[1,1,512,128]{3,2,1,0:T(8,128)(2,1)S(1)} %collective-permute-done) | copy-start | bytes 393220
  16.6 9.9 %copy-start.15 = (bf16[1,1,512,128]{3,2,1,0:T(8,128)(2,1)}, bf16[1,1,512,128]{3,2,1,0:T(8,128)(2,1)S(1)}, u32[]{:S(2)}) copy-start(bf16[1,1,512,128]{3,2,1,0:T(8,128)(2,1)S(1)} %collective-permute-done.1) | copy-start | bytes 393220
  19.3 8.0 %copy-start.1 = (bf16[1,18,514,128]{3,2,1,0:T(8,128)(2,1)}, bf16[1,18,514,128]{3,2,1,0:T(8,128)(2,1)S(1)}, u32[]{:S(2)}) copy-start(bf16[1,18,514,128]{3,2,1,0:T(8,128)(2,1)S(1)} %fusion.10) | copy-start | bytes 7105540
  27.3 5.3 %copy-start.9 = (f32[512,128]{1,0:T(8,128)S(1)}, f32[512,128]{1,0:T(8,128)}, u32[]{:S(2)}) copy-start(f32[512,128]{1,0:T(8,128)} %param.11) | copy-start | bytes 786436
  29.0 255.9 %all-reduce.3.cloned.1.call-start = ((), (), s32[]{:S(2)}) async-start(), calls=%async_computation.2 | async-start | bytes 524288 | tf_op jit(solution)/shard_map/psum | solution.py:87
  32.6 3.6 copy-start.37
  120.7 3.8 copy-start.25
  123.0 8.2 %copy-start.8 = (f32[9,128,128]{2,1,0:T(8,128)}, f32[9,128,128]{2,1,0:T(8,128)S(1)}, u32[]{:S(2)}) copy-start(f32[9,128,128]{2,1,0:T(8,128)S(1)} %get-tuple-element.17) | copy-start | bytes 1769476
  137.8 3.7 copy-start.18
  141.5 4.8 %copy-start.27 = (f32[128]{0:T(128)S(1)}, f32[128]{0:T(128)}, u32[]{:S(2)}) copy-start(f32[128]{0:T(128)} %fusion.128) | copy-start | bytes 1540
  142.2 4.1 %copy-start.36 = (f32[128]{0:T(128)S(1)}, f32[128]{0:T(128)}, u32[]{:S(2)}) copy-start(f32[128]{0:T(128)} %convolution_bitcast_fusion) | copy-start | bytes 1540
  143.5 3.5 copy-start.31
  143.5 3.5 copy-start.40
  143.5 3.5 copy-start.6
  143.5 3.5 copy-start.38
  149.4 249.1 %reduce-scatter.2.cloned.1.call-start = ((), (), s32[]{:S(2)}) async-start(), calls=%async_computation.1 | async-start | bytes 5013504 | tf_op jit(solution)/shard_map/reduce_scatter | solution.py:86
  153.7 10.7 %copy-start.34 = (f32[8]{0:T(128)S(1)}, f32[8]{0:T(128)}, u32[]{:S(2)}) copy-start(f32[8]{0:T(128)} %copy-done.33) | copy-start | bytes 100
  153.7 73.8 %copy-start.11 = (bf16[1,9,128,128]{3,2,1,0:T(8,128)(2,1)S(1)}, bf16[1,9,128,128]{3,2,1,0:T(8,128)(2,1)}, u32[]{:S(2)}) copy-start(bf16[1,9,128,128]{3,2,1,0:T(8,128)(2,1)} %get-tuple-element.22) | copy-start | bytes 884740
  153.7 73.8 %copy-start.16 = (bf16[1,1,512,128]{3,2,1,0:T(8,128)(2,1)S(1)}, bf16[1,1,512,128]{3,2,1,0:T(8,128)(2,1)}, u32[]{:S(2)}) copy-start(bf16[1,1,512,128]{3,2,1,0:T(8,128)(2,1)} %copy-done.15) | copy-start | bytes 393220
  (22 other events, 40.5 us)
Sparse Core Ops, SparseCore 0:
  29.1 87.1 all-gather.2
  149.5 135.2 all-reduce.2
  288.2 110.2 reduce-scatter.1
